TPU v7x, 256 devices: a whole 4x4x8 slice. The times are simulated.
256 devices in a mesh: leaf: 2 (over core), row: 16 (over y, x), col: 8 (over z).
Axes of the slice: x: 4, y: 4, z: 8, core: 2. Of those that a mesh axis runs over, the one named last changes fastest.
Arguments:
- ancestor_inverse: bfloat16 [16384, 16384], P(('leaf', 'col'), 'row'), may hold values from -6 to 6
- panels: bfloat16 [16384, 4096], P('row', ('leaf', 'col')), may hold values from -0.046875 to 0.046875
- pattern: int32 [64, 16], replicated, may hold values from 0 to 1
- diag_inverse: float32 [16, 256, 256], P('row'), may hold values from -6 to 6
Outputs:
- covariance: float32 [16384, 4096], P(('leaf', 'col'), 'row')
- diag_cov: float32 [16, 256, 256], P('row')
All inputs are finite; a program needn't handle non-finite values.
Results may differ from a plain program's by a relative error of at most 0.0003.
Values may be sent and summed in bfloat16 or wider, within the bound.
A program may use at most 128 MiB of HBM per device.

v0:
```python
import jax
import jax.numpy as jnp
from jax import lax
from jax.sharding import PartitionSpec as P


def local(ancestor_inverse, panels, pattern, diag_inverse):
    block_width = diag_inverse.shape[1]
    n_leaf = lax.axis_size("leaf")
    n_row = lax.axis_size("row")
    n_col = lax.axis_size("col")
    ancestors = pattern.shape[0]
    supers = pattern.shape[1]
    groups = n_leaf * n_col
    group_pos = lax.axis_index("leaf") * n_col + lax.axis_index("col")
    row_pos = lax.axis_index("row")
    blocks_native = ancestors // n_row
    sups_native = supers // groups
    native_pattern = lax.dynamic_slice(
        pattern, (row_pos * blocks_native, group_pos * sups_native), (blocks_native, sups_native)
    )
    shaped = panels.reshape(blocks_native, block_width, sups_native, block_width)
    masked = (shaped * native_pattern[:, None, :, None].astype(jnp.bfloat16)).reshape(panels.shape)
    gathered = lax.all_gather(masked, ("leaf", "col"), axis=1, tiled=True)
    partial_sum = jnp.dot(ancestor_inverse, gathered, preferred_element_type=jnp.float32)
    product = lax.psum_scatter(partial_sum, "row", scatter_dimension=1, tiled=True)
    blocks_out = ancestors // groups
    rows_group = blocks_out * block_width
    sups_out = supers // n_row
    exchanged = lax.all_to_all(gathered, "row", split_axis=1, concat_axis=0, tiled=True)
    matching = lax.dynamic_slice_in_dim(exchanged, group_pos * rows_group, rows_group, 0)
    out_pattern = lax.dynamic_slice(
        pattern, (group_pos * blocks_out, row_pos * sups_out), (blocks_out, sups_out)
    )
    product_blocks = product.reshape(blocks_out, block_width, sups_out, block_width)
    covariance = -(product_blocks * out_pattern[:, None, :, None].astype(jnp.float32)).reshape(
        product.shape
    )
    columns = matching.astype(jnp.float32).reshape(rows_group, sups_out, block_width)
    results = product.reshape(rows_group, sups_out, block_width)
    local_terms = jnp.einsum("nsa,nsb->sab", columns, results, precision=lax.Precision.HIGHEST)
    summed_terms = lax.psum(local_terms, ("leaf", "col"))
    diag_cov = diag_inverse + summed_terms
    return (covariance, diag_cov)


def solution(mesh):
    placed = (P(("leaf", "col"), "row"), P("row", ("leaf", "col")), P(), P("row", None, None))
    return jax.shard_map(
        local,
        mesh=mesh,
        in_specs=placed,
        out_specs=(P(("leaf", "col"), "row"), P("row", None, None)),
        check_vma=False,
    )
```

profile of v0, /device:TPU:1, one launch (start us, length us, event | category | flops | bytes accessed | tf_op | source)
XLA Modules:
  0.0 425.0 jit_solution(16035267474393045145)
XLA Ops:
  7.2 0.0 copy-start
  7.2 0.0 all-gather.2.cloned.1.call-start
  7.2 0.9 convert_bitcast_fusion
  8.2 0.1 broadcast_bitcast_fusion.1
  8.2 1.2 copy.8
  9.5 0.8 broadcast_multiply_fusion
  10.3 0.0 all-gather.2.cloned.1.call-update
  10.3 0.0 reduce-scatter.2.cloned.1.call-start
  10.4 60.2 %all-gather.2.cloned.1.call-done = bf16[1024,4096]{0,1:T(8,128)(2,1)} async-done(((bf16[1024,256]{0,1:T(8,128)(2,1)}), bf16[1024,4096]{0,1:T(8,128)(2,1)}) %all-gather.2.cloned.1.call-update) | async-done | bytes 8388624 | tf_op jit(solution)/shard_map/all_gather | solution.py:24
  70.6 0.0 copy-done
  70.6 14.6 %convolution_bitcast_fusion = f32[1024,4096]{0,1:T(8,128)} fusion(bf16[1024,4096]{0,1:T(8,128)(2,1)} %all-gather.2.cloned.1.call-done, bf16[1024,1024]{1,0:T(8,128)(2,1)S(1)} %copy-done), kind=kOutput, calls=%fused_computation | convolution fusion | flops 8589934592 | bytes 27262976 | tf_op jit(solution)/shard_map/dot_general | solution.py:25
  85.2 0.0 reduce-scatter.2.cloned.1.call-update
  85.2 6.6 %all-to-all-start = ((bf16[1024,16,256]{0,2,1:T(8,128)(2,1)}), bf16[1024,16,256]{0,2,1:T(8,128)(2,1)}, u32[]{:S(2)}, u32[]{:S(2)}) async-start(bf16[1024,16,256]{0,2,1:T(8,128)(2,1)} %bitcast.21), calls=%async_computation.1 | async-start | bytes 16777216 | tf_op jit(solution)/shard_map/all_to_all | solution.py:30
  91.8 0.0 all-reduce.2.cloned.1.call-start
  91.9 0.1 broadcast_bitcast_fusion
  92.0 151.2 %all-to-all-done = bf16[1024,16,256]{0,2,1:T(8,128)(2,1)} async-done(((bf16[1024,16,256]{0,2,1:T(8,128)(2,1)}), bf16[1024,16,256]{0,2,1:T(8,128)(2,1)}, u32[]{:S(2)}, u32[]{:S(2)}) %all-to-all-start) | async-done | bytes 8388640 | tf_op jit(solution)/shard_map/all_to_all | solution.py:30
  243.2 0.0 copy-start.1
  243.2 12.4 %copy.9 = bf16[16,1024,256]{2,1,0:T(8,128)(2,1)} copy(bf16[16,1024,256]{1,2,0:T(8,128)(2,1)} %bitcast.4) | data formatting | bytes 16777216 | tf_op jit(solution)/shard_map/all_to_all | solution.py:30
  255.6 49.5 %reduce-scatter.2.cloned.1.call-done = f32[1024,256]{0,1:T(8,128)} async-done(((f32[1024,4096]{0,1:T(8,128)}), f32[1024,256]{0,1:T(8,128)}) %reduce-scatter.2.cloned.1.call-update) | async-done | bytes 1048592 | tf_op jit(solution)/shard_map/reduce_scatter | solution.py:26
  305.1 2.9 convolution_bitcast_fusion.1
  308.0 0.0 all-reduce.2.cloned.1.call-update
  308.0 1.3 multiply_negate_fusion
  309.4 1.3 copy.10
  310.7 106.1 %all-reduce.2.cloned.1.call-done = f32[1,256,256]{2,1,0:T(8,128)} async-done(((f32[1,256,256]{2,1,0:T(8,128)}), f32[1,256,256]{2,1,0:T(8,128)}) %all-reduce.2.cloned.1.call-update) | async-done | bytes 262160 | tf_op jit(solution)/shard_map/psum | solution.py:42
  416.8 0.0 copy-done.1
  416.8 1.7 add.31
  (2 shorter events, 0.0 us)
Async XLA Ops:
  7.2 63.5 %copy-start = (bf16[1024,1024]{1,0:T(8,128)(2,1)S(1)}, bf16[1024,1024]{1,0:T(8,128)(2,1)}, u32[]{:S(2)}) copy-start(bf16[1024,1024]{1,0:T(8,128)(2,1)} %param.4) | copy-start | bytes 6291460
  7.2 63.5 %all-gather.2.cloned.1.call-start = ((), (), s32[]{:S(2)}) async-start(), calls=%async_computation.2 | async-start | bytes 8912896 | tf_op jit(solution)/shard_map/all_gather | solution.py:24
  10.3 294.8 %reduce-scatter.2.cloned.1.call-start = ((), (), s32[]{:S(2)}) async-start(), calls=%async_computation.3 | async-start | bytes 17825792 | tf_op jit(solution)/shard_map/reduce_scatter | solution.py:26
  85.2 158.0 %all-to-all-start = ((bf16[1024,16,256]{0,2,1:T(8,128)(2,1)}), bf16[1024,16,256]{0,2,1:T(8,128)(2,1)}, u32[]{:S(2)}, u32[]{:S(2)}) async-start(bf16[1024,16,256]{0,2,1:T(8,128)(2,1)} %bitcast.21), calls=%async_computation.1 | async-start | bytes 16777216 | tf_op jit(solution)/shard_map/all_to_all | solution.py:30
  91.8 324.9 %all-reduce.2.cloned.1.call-start = ((), (), s32[]{:S(2)}) async-start(), calls=%async_computation.4 | async-start | bytes 524288 | tf_op jit(solution)/shard_map/psum | solution.py:42
  243.2 173.6 %copy-start.1 = (f32[1,256,256]{2,1,0:T(8,128)S(1)}, f32[1,256,256]{2,1,0:T(8,128)}, u32[]{:S(2)}) copy-start(f32[1,256,256]{2,1,0:T(8,128)} %param.7) | copy-start | bytes 786436
Sparse Core Ops, SparseCore 0:
  10.5 60.1 all-gather.1
  85.3 219.7 reduce-scatter.1
  308.1 108.5 all-reduce.1
where the time goes:
time: 426 us; the launch traced here: 425 us
  waiting for transfers between devices  367 us (86%)
  matrix products  17.4 us (4%)
  local copies, waits for them, and re-layouts  15.1 us (4%)
  between operations  13.8 us (3%)
  starting transfers between devices  6.71 us (2%)
  other arithmetic  4.77 us (1%)
    all_to_all x1, waiting for transfers between devices, local(): lax.all_to_all(gathered, 'row', split_axis=1, concat_axis=0, tiled=True)  151 us
    psum x1, waiting for transfers between devices, local(): summed_terms = lax.psum(local_terms, ('leaf', 'col'))  106 us
    all_gather x1, waiting for transfers between devices, local(): gathered = lax.all_gather(masked, ('leaf', 'col'), axis=1, tiled=True)  60.2 us
    reduce_scatter x1, waiting for transfers between devices, local(): lax.psum_scatter(partial_sum, 'row', scatter_dimension=1, tiled=True)  49.5 us
    dot_general x1, matrix products, local(): jnp.dot(ancestor_inverse, gathered, preferred_element_type=jnp.float32)  14.6 us
    all_to_all x1, local copies, waits for them, and re-layouts, local(): lax.all_to_all(gathered, 'row', split_axis=1, concat_axis=0, tiled=True)  12.4 us
  transfers between devices with their start and end apart: 4, of which 4 were waited for; matrix products, arithmetic and copies ran while one was open for 4% of the time, Pallas kernels for 0%

commit v1 on v0

v1 whole, which is shorter than its diff:
```python
import jax
import jax.numpy as jnp
from jax import lax
from jax.experimental import pallas as pl
from jax.experimental.pallas import tpu as pltpu
from jax.sharding import PartitionSpec as P

MESH = pl.DeviceIdType.MESH
SIDE = 4
LANES = 128
OFFSETS = (2, 1, 3, 0)


def kernel(
    pattern, a_ref, panel, dinv, cov, diag,
    mbuf, match, pbuf, r1, r2, r3, r4, term, dpart, dsum,
    zs, zr, ls, lr, s1, q1, s2, q2, s3, q3, s4, q4, ts, tr, ps, pr, bs, br,
):
    nz = lax.axis_size("col")
    leaf = lax.axis_index("leaf")
    row = lax.axis_index("row")
    z = lax.axis_index("col")
    y = row // SIDE
    x = lax.rem(row, SIDE)
    groups = 2 * nz
    group = leaf * nz + z
    depth = panel.shape[0]
    block = dinv.shape[1]
    blocks = depth // block
    half = depth // 2
    quarter = depth // 4
    chunks = block // LANES
    piece = block // groups

    def peer(j):
        p = lax.rem(group + j, groups)
        return (p // nz, row, lax.rem(p, nz))

    def z_dev(step):
        return (leaf, row, lax.rem(z + step + nz, nz))

    def x_dev(step):
        return (leaf, y * SIDE + lax.rem(x + step + SIDE, SIDE), z)

    def y_dev(step):
        return (leaf, lax.rem(y + step + SIDE, SIDE) * SIDE + x, z)

    other = (1 - leaf, row, z)
    swapped = (row // nz, group, lax.rem(row, nz))
    moves = row != group

    def remote(src, dst, send, recv, dev):
        return pltpu.make_async_remote_copy(
            src_ref=src, dst_ref=dst, send_sem=send, recv_sem=recv,
            device_id=dev, device_id_type=MESH,
        )

    barrier = pltpu.get_barrier_semaphore()

    @pl.loop(1, groups)
    def _(j):
        pl.semaphore_signal(barrier, inc=1, device_id=peer(j), device_id_type=MESH)

    for dev in (x_dev(1), x_dev(-1), y_dev(1), y_dev(-1)):
        pl.semaphore_signal(barrier, inc=1, device_id=dev, device_id_type=MESH)

    @pl.when(moves)
    def _():
        pl.semaphore_signal(barrier, inc=1, device_id=swapped, device_id_type=MESH)

    for c in range(chunks):
        for i in range(blocks):
            keep = pattern[row * blocks + i, group].astype(jnp.float32)
            rows = pl.ds(i * block, block)
            values = panel[rows, pl.ds(c * LANES, LANES)].astype(jnp.float32) * keep
            mbuf[c, group, rows, :] = values.astype(jnp.bfloat16)

    pl.semaphore_wait(barrier, groups - 1 + 4 + moves.astype(jnp.int32))

    turns = nz // 2
    pieces = 2 * turns - 1

    def z_rows(way, j):
        h = j % 2 if way == 0 else 1 - j % 2
        return pl.ds(h * half, half)

    def z_copy(c, way, j, lag):
        step = -1 if way == 0 else 1
        s = leaf * nz + lax.rem(z + step * (j // 2 + lag) + 2 * nz, nz)
        view = mbuf.at[c, s, z_rows(way, j), :]
        return remote(view, view, zs.at[c, way, j], zr.at[c, way, j], z_dev(-step))

    def leaf_copy(c, way, j, lf):
        step = -1 if way == 0 else 1
        s = lf * nz + lax.rem(z + step * (j // 2 + 1) + 2 * nz, nz)
        view = mbuf.at[c, s, z_rows(way, j), :]
        n = way * pieces + j
        return remote(view, view, ls.at[c, n], lr.at[c, n], other)

    def leaf_own(c, lf):
        view = mbuf.at[c, lf * nz + z]
        return remote(view, view, ls.at[c, 2 * pieces], lr.at[c, 2 * pieces], other)

    def gather_begin(c):
        for j in range(2):
            for way in range(2):
                z_copy(c, way, j, 0).start()
        leaf_own(c, leaf).start()

    def gather_step(c, d):
        for j in range(2 * d, min(2 * d + 2, pieces)):
            for way in range(2):
                z_copy(c, way, j, 1).wait_recv()
                if j + 2 < pieces:
                    z_copy(c, way, j + 2, 0).start()
                leaf_copy(c, way, j, leaf).start()

    def multiply(c, sa, sb):
        @pl.loop(0, a_ref.shape[0] // 256)
        def _(t):
            rows = pl.ds(pl.multiple_of(t * 256, 256), 256)
            right = jnp.concatenate([mbuf[c, sa], mbuf[c, sb]], axis=1)
            out = jnp.dot(a_ref[rows, :], right, preferred_element_type=jnp.float32)
            pbuf[c, sa, rows, :] = out[:, :LANES]
            pbuf[c, sb, rows, :] = out[:, LANES:]

    def products(c, d):
        if d == 0:
            leaf_own(c, 1 - leaf).wait_recv()
            multiply(c, leaf * nz + z, (1 - leaf) * nz + z)
            return
        for j in range(2 * d - 2, min(2 * d, pieces)):
            for way in range(2):
                leaf_copy(c, way, j, 1 - leaf).wait_recv()
        up = lax.rem(z + d, nz)
        down = lax.rem(z + nz - d, nz)
        if d == turns:
            multiply(c, leaf * nz + up, (1 - leaf) * nz + up)
        else:
            multiply(c, leaf * nz + up, leaf * nz + down)
            multiply(c, (1 - leaf) * nz + up, (1 - leaf) * nz + down)

    def first(f):
        return (x, y)[f]

    def second(f):
        return (y, x)[f]

    def dev_first(f, step):
        return (x_dev, y_dev)[f](step)

    def dev_second(f, step):
        return (y_dev, x_dev)[f](step)

    def part(c, f, df, k, lo, n):
        a = lax.rem(first(f) + df, SIDE)
        b = lax.rem(second(f) + OFFSETS[k], SIDE)
        s = b * SIDE + a if f == 0 else a * SIDE + b
        return pbuf.at[c, s, pl.ds(f * half + lo, n), :]

    def far(c, f, way, k):
        return remote(
            part(c, f, 2, k, way * quarter, quarter), r1.at[c, f, way, k],
            s1.at[c, f, way, k], q1.at[c, f, way, k], dev_first(f, 1 - 2 * way),
        )

    def near(c, f, way, k):
        return remote(
            part(c, f, 1 + 2 * way, k, 0, half), r2.at[c, f, way, k],
            s2.at[c, f, way, k], q2.at[c, f, way, k], dev_first(f, 1 - 2 * way),
        )

    def far_second(c, f, way):
        return remote(
            part(c, f, 0, 0, way * quarter, quarter), r3.at[c, f, way],
            s3.at[c, f, way], q3.at[c, f, way], dev_second(f, 1 - 2 * way),
        )

    def near_second(c, f, way):
        return remote(
            part(c, f, 0, 1 + way, 0, half), r4.at[c, f, way],
            s4.at[c, f, way], q4.at[c, f, way], dev_second(f, 1 - 2 * way),
        )

    def send_far(c, k):
        for f in range(2):
            for way in range(2):
                far(c, f, way, k).start()

    def send_near(c, k):
        for f in range(2):
            for way in range(2):
                far(c, f, way, k).wait_recv()
                own = part(c, f, 1 + 2 * way, k, way * quarter, quarter)
                own[...] = own[...] + r1[c, f, way, k]
                near(c, f, way, k).start()

    def turn(c, k):
        for f in range(2):
            for way in range(2):
                near(c, f, way, k).wait_recv()
            own = part(c, f, 0, k, 0, half)
            own[...] = own[...] + (r2[c, f, 0, k] + r2[c, f, 1, k])
            if k == 0:
                far_second(c, f, 0).start()
                far_second(c, f, 1).start()
            elif k < 3:
                way = k - 1
                far_second(c, f, way).wait_recv()
                own = part(c, f, 0, k, way * quarter, quarter)
                own[...] = own[...] + r3[c, f, way]
                near_second(c, f, way).start()

    def swap(c):
        return remote(mbuf.at[c, group], match.at[c], ts.at[c], tr.at[c], swapped)

    def finish(c):
        for f in range(2):
            for way in range(2):
                near_second(c, f, way).wait_recv()
            own = part(c, f, 0, 3, 0, half)
            own[...] = own[...] + (r4[c, f, 0] + r4[c, f, 1])
        product = pbuf.at[c, row]

        if c == 0:
            @pl.when(moves)
            def _():
                for e in range(chunks):
                    swap(e).wait_recv()

        value = product[...]
        total = None
        rest = value
        columns = jnp.concatenate([match[e] for e in range(chunks)], axis=1)
        for _ in range(3):
            top = rest.astype(jnp.bfloat16)
            rest = rest - top.astype(jnp.float32)
            add = lax.dot_general(
                columns, top, (((0,), (0,)), ((), ())), preferred_element_type=jnp.float32
            )
            total = add if total is None else total + add
        term[c] = total

        @pl.loop(1, groups)
        def _(j):
            give(c, j).start()

        for i in range(blocks):
            keep = pattern[group * blocks + i, row].astype(jnp.float32)
            rows = pl.ds(i * block, block)
            cov[rows, pl.ds(c * LANES, LANES)] = -(product[rows, :] * keep)

    def give(c, j):
        to = lax.rem(group + j, groups)
        rows = pl.ds(pl.multiple_of(to * piece, piece), piece)
        return remote(term.at[c, rows, :], dpart.at[c, j], ps.at[c, j], pr.at[c, j], peer(j))

    def mine(owner):
        return pl.ds(pl.multiple_of(owner * piece, piece), piece)

    def spread(c, j, owner):
        view = dsum.at[c, mine(owner), :]
        return remote(view, view, bs.at[c, j], br.at[c, j], peer(j))

    def settle(c):
        @pl.loop(1, groups)
        def _(j):
            give(c, j).wait_recv()

        dsum[c, mine(group), :] = (
            dinv[0, mine(group), pl.ds(c * LANES, LANES)]
            + (term[c, mine(group), :] + jnp.sum(dpart[c, pl.ds(1, groups - 1)], axis=0))
        )

        @pl.loop(1, groups)
        def _(j):
            spread(c, j, group).start()

    def collect(c):
        @pl.loop(1, groups)
        def _(j):
            spread(c, j, lax.rem(group - j + groups, groups)).wait_recv()

        diag[0, :, pl.ds(c * LANES, LANES)] = dsum[c]

    gather_begin(0)
    products(0, 0)
    for d in range(turns):
        gather_step(0, d)
        if d == turns - 2:
            gather_begin(1)
            @pl.when(moves)
            def _():
                for c in range(chunks):
                    swap(c).start()

            @pl.when(jnp.logical_not(moves))
            def _():
                for c in range(chunks):
                    match[c] = mbuf[c, group]
        if d > 0:
            products(0, d)
    products(0, turns)
    for k in range(4):
        send_far(0, k)
    products(1, 0)
    for k in range(4):
        gather_step(1, k)
        send_near(0, k)
        products(1, k + 1)
    for k in range(4):
        send_far(1, k)
    for k in range(4):
        turn(0, k)
        send_near(1, k)
    finish(0)
    for k in range(4):
        turn(1, k)
    settle(0)
    finish(1)
    collect(0)
    settle(1)
    collect(1)

    for c in range(chunks):
        leaf_own(c, leaf).wait_send()
        for way in range(2):
            for j in range(pieces):
                z_copy(c, way, j, 0).wait_send()
                leaf_copy(c, way, j, leaf).wait_send()
            for f in range(2):
                for k in range(4):
                    far(c, f, way, k).wait_send()
                    near(c, f, way, k).wait_send()
                far_second(c, f, way).wait_send()
                near_second(c, f, way).wait_send()

        @pl.loop(1, groups)
        def _(j):
            give(c, j).wait_send()
            spread(c, j, group).wait_send()

        @pl.when(moves)
        def _():
            swap(c).wait_send()


def local(ancestor_inverse, panels, pattern, diag_inverse):
    depth, width = panels.shape
    rows_out = ancestor_inverse.shape[0]
    block = diag_inverse.shape[1]
    nz = lax.axis_size("col")
    groups = 2 * nz
    supers = pattern.shape[1]
    chunks = block // LANES
    half, quarter = depth // 2, depth // 4
    f32, bf16 = jnp.float32, jnp.bfloat16
    pieces = 2 * (nz // 2) - 1
    dma = pltpu.SemaphoreType.DMA
    vmem = pl.BlockSpec(memory_space=pltpu.VMEM)
    sems = [
        (chunks, 2, pieces), (chunks, 2 * pieces + 1),
        (chunks, 2, 2, 4), (chunks, 2, 2, 4), (chunks, 2, 2), (chunks, 2, 2),
        (chunks,), (chunks, groups), (chunks, groups),
    ]
    return tuple(pl.pallas_call(
        kernel,
        out_shape=(
            jax.ShapeDtypeStruct((rows_out, width), f32),
            jax.ShapeDtypeStruct(diag_inverse.shape, f32),
        ),
        in_specs=[pl.BlockSpec(memory_space=pltpu.SMEM), vmem, vmem, vmem],
        out_specs=(vmem, vmem),
        scratch_shapes=[
            pltpu.VMEM((chunks, supers, depth, LANES), bf16),
            pltpu.VMEM((chunks, depth, LANES), bf16),
            pltpu.VMEM((chunks, supers, rows_out, LANES), f32),
            pltpu.VMEM((chunks, 2, 2, 4, quarter, LANES), f32),
            pltpu.VMEM((chunks, 2, 2, 4, half, LANES), f32),
            pltpu.VMEM((chunks, 2, 2, quarter, LANES), f32),
            pltpu.VMEM((chunks, 2, 2, half, LANES), f32),
            pltpu.VMEM((chunks, block, LANES), f32),
            pltpu.VMEM((chunks, groups, block // groups, LANES), f32),
            pltpu.VMEM((chunks, block, LANES), f32),
        ] + [dma(s) for s in sems for _ in range(2)],
        compiler_params=pltpu.CompilerParams(
            collective_id=0, has_side_effects=True, vmem_limit_bytes=58 * 2**20
        ),
        cost_estimate=pl.CostEstimate(
            flops=2 * rows_out * depth * supers * block, bytes_accessed=8 * 2**20, transcendentals=0
        ),
    )(pattern, ancestor_inverse, panels, diag_inverse))


def solution(mesh):
    placed = (P(("leaf", "col"), "row"), P("row", ("leaf", "col")), P(), P("row", None, None))
    return jax.shard_map(
        local,
        mesh=mesh,
        in_specs=placed,
        out_specs=(P(("leaf", "col"), "row"), P("row", None, None)),
        check_vma=False,
    )
```

time: 426 us -> 192 us (0.45)
  waiting for transfers between devices: 367 us -> 0 us
  Pallas kernels: 0 us -> 186 us
  matrix products: 17.4 us -> 0 us
  between operations: 13.8 us -> 0.65 us
  local copies, waits for them, and re-layouts: 15.1 us -> 4.41 us
  starting transfers between devices: 6.71 us -> 0 us
  other arithmetic: 4.77 us -> 0 us
    pallas_call x0 -> x1, Pallas kernels: none -> 186 us  [local(): pl.pallas_call(kernel, out_shape=(jax.ShapeDtypeStruct((rows_out, width),...]
    all_to_all x1 -> x0, waiting for transfers between devices: 151 us -> none  [local(): lax.all_to_all(gathered, 'row', split_axis=1, concat_axis=0, tiled=True)]
    psum x1 -> x0, waiting for transfers between devices: 106 us -> none  [local(): summed_terms = lax.psum(local_terms, ('leaf', 'col'))]
    all_gather x1 -> x0, waiting for transfers between devices: 60.2 us -> none  [local(): gathered = lax.all_gather(masked, ('leaf', 'col'), axis=1, tiled=True)]
    reduce_scatter x1 -> x0, waiting for transfers between devices: 49.5 us -> none  [local(): lax.psum_scatter(partial_sum, 'row', scatter_dimension=1, tiled=True)]
    dot_general x2 -> x0, matrix products: 17.4 us -> none  [the longest x1 14.6 us: local(): jnp.dot(ancestor_inverse, gathered, preferred_element_type=jnp.float32)]
    all_to_all x1 -> x0, local copies, waits for them, and re-layouts: 12.4 us -> none  [local(): lax.all_to_all(gathered, 'row', split_axis=1, concat_axis=0, tiled=True)]
    all_to_all x1 -> x0, starting transfers between devices: 6.59 us -> none  [local(): lax.all_to_all(gathered, 'row', split_axis=1, concat_axis=0, tiled=True)]
  transfers between devices with their start and end apart: 4 -> 0, of which waited for: 4 -> 0; matrix products, arithmetic and copies ran while one was open for 4% -> 0% of each run, Pallas kernels for 0% -> 0%
where the time goes in v1:
time: 192 us; the launch traced here: 191 us
  Pallas kernels  186 us (97%)
  local copies, waits for them, and re-layouts  4.41 us (2%)
    pallas_call x1, Pallas kernels, local(): pl.pallas_call(kernel, out_shape=(jax.ShapeDtypeStruct((rows_out, width),...  186 us
    unnamed x5, local copies, waits for them, and re-layouts  4.41 us

profile of v1, /device:TPU:1, one launch (start us, length us, event | category | flops | bytes accessed | tf_op | source)
XLA Modules:
  0.0 191.4 jit_solution(3513850261101076326)
XLA Ops:
  0.6 1.4 copy.6.pattern
  2.0 186.3 %shard_map.59 = (f32[1024,256]{1,0:T(8,128)}, f32[1,256,256]{2,1,0:T(8,128)}) custom-call(s32[64,16]{1,0:T(8,128)} %copy.6.pattern, bf16[1024,1024]{1,0:T(8,128)(2,1)} %a_ref.1, bf16[1024,256]{1,0:T(8,128)(2,1)} %panel.1, f32[1,256,256]{2,1,0:T(8,128)} %dinv.1), custom_call_target="tpu_custom_call" | custom-call | flops 8589934592 | bytes 8388608 | tf_op jit(solution)/shard_map/pallas_call | solution.py:366
  188.4 0.0 copy-start
  188.4 2.3 %copy.9 = f32[1024,256]{1,0:T(8,128)} copy(f32[1024,256]{1,0:T(8,128)} %get-tuple-element.4) | data formatting | bytes 2097152
  190.7 0.0 copy-done
  190.7 0.7 copy.10
Async XLA Ops:
  188.4 2.3 %copy-start = (f32[1,256,256]{2,1,0:T(8,128)S(1)}, f32[1,256,256]{2,1,0:T(8,128)}, u32[]{:S(2)}) copy-start(f32[1,256,256]{2,1,0:T(8,128)} %get-tuple-element.5) | copy-start | bytes 786436

commit v2 on v1

--- a/solution.py
+++ b/solution.py
@@ -13,7 +13,7 @@
 
 def kernel(
     pattern, a_ref, panel, dinv, cov, diag,
-    mbuf, match, pbuf, r1, r2, r3, r4, term, dpart, dsum,
+    mbuf, match, relay, pbuf, r1, r2, r3, r4, term, dpart, dsum,
     zs, zr, ls, lr, s1, q1, s2, q2, s3, q3, s4, q4, ts, tr, ps, pr, bs, br,
 ):
     nz = lax.axis_size("col")
@@ -46,8 +46,13 @@
         return (leaf, lax.rem(y + step + SIDE, SIDE) * SIDE + x, z)
 
     other = (1 - leaf, row, z)
-    swapped = (row // nz, group, lax.rem(row, nz))
-    moves = row != group
+    held = leaf * nz + lax.rem(z + 2 * leaf + row, nz)
+    taker = (row // nz, held, z)
+    turned = lax.rem(row - z - 2 * (row // nz) + 2 * nz, nz)
+    giver = (row // nz, leaf * nz + turned, z)
+    moves = jnp.logical_or(row // nz != leaf, held != row)
+    onward = (leaf, row, turned)
+    goes_on = turned != z
 
     def remote(src, dst, send, recv, dev):
         return pltpu.make_async_remote_copy(
@@ -66,11 +71,11 @@
 
     @pl.when(moves)
     def _():
-        pl.semaphore_signal(barrier, inc=1, device_id=swapped, device_id_type=MESH)
+        pl.semaphore_signal(barrier, inc=1, device_id=giver, device_id_type=MESH)
 
     for c in range(chunks):
         for i in range(blocks):
-            keep = pattern[row * blocks + i, group].astype(jnp.float32)
+            keep = pattern[group, row * blocks + i].astype(jnp.float32)
             rows = pl.ds(i * block, block)
             values = panel[rows, pl.ds(c * LANES, LANES)].astype(jnp.float32) * keep
             mbuf[c, group, rows, :] = values.astype(jnp.bfloat16)
@@ -212,7 +217,32 @@
                 near_second(c, f, way).start()
 
     def swap(c):
-        return remote(mbuf.at[c, group], match.at[c], ts.at[c], tr.at[c], swapped)
+        return remote(mbuf.at[c, held], relay.at[c], ts.at[c, 0], tr.at[c, 0], taker)
+
+    def swap_on(c):
+        return remote(relay.at[c], match.at[c], ts.at[c, 1], tr.at[c, 1], onward)
+
+    def send_match(c):
+        @pl.when(moves)
+        def _():
+            swap(c).start()
+
+        @pl.when(jnp.logical_not(moves))
+        def _():
+            relay[c] = mbuf[c, held]
+
+    def pass_match(c):
+        @pl.when(moves)
+        def _():
+            swap(c).wait_recv()
+
+        @pl.when(goes_on)
+        def _():
+            swap_on(c).start()
+
+        @pl.when(jnp.logical_not(goes_on))
+        def _():
+            match[c] = relay[c]
 
     def finish(c):
         for f in range(2):
@@ -223,10 +253,10 @@
         product = pbuf.at[c, row]
 
         if c == 0:
-            @pl.when(moves)
+            @pl.when(goes_on)
             def _():
                 for e in range(chunks):
-                    swap(e).wait_recv()
+                    swap_on(e).wait_recv()
 
         value = product[...]
         total = None
@@ -246,7 +276,7 @@
             give(c, j).start()
 
         for i in range(blocks):
-            keep = pattern[group * blocks + i, row].astype(jnp.float32)
+            keep = pattern[row, group * blocks + i].astype(jnp.float32)
             rows = pl.ds(i * block, block)
             cov[rows, pl.ds(c * LANES, LANES)] = -(product[rows, :] * keep)
 
@@ -289,30 +319,25 @@
         gather_step(0, d)
         if d == turns - 2:
             gather_begin(1)
-            @pl.when(moves)
-            def _():
-                for c in range(chunks):
-                    swap(c).start()
-
-            @pl.when(jnp.logical_not(moves))
-            def _():
-                for c in range(chunks):
-                    match[c] = mbuf[c, group]
         if d > 0:
             products(0, d)
     products(0, turns)
     for k in range(4):
         send_far(0, k)
+    send_match(0)
     products(1, 0)
     for k in range(4):
         gather_step(1, k)
         send_near(0, k)
         products(1, k + 1)
+    pass_match(0)
     for k in range(4):
         send_far(1, k)
+    send_match(1)
     for k in range(4):
         turn(0, k)
         send_near(1, k)
+    pass_match(1)
     finish(0)
     for k in range(4):
         turn(1, k)
@@ -344,6 +369,10 @@
         def _():
             swap(c).wait_send()
 
+        @pl.when(goes_on)
+        def _():
+            swap_on(c).wait_send()
+
 
 def local(ancestor_inverse, panels, pattern, diag_inverse):
     depth, width = panels.shape
@@ -352,6 +381,7 @@
     nz = lax.axis_size("col")
     groups = 2 * nz
     supers = pattern.shape[1]
+    turned = pattern.T
     chunks = block // LANES
     half, quarter = depth // 2, depth // 4
     f32, bf16 = jnp.float32, jnp.bfloat16
@@ -361,7 +391,7 @@
     sems = [
         (chunks, 2, pieces), (chunks, 2 * pieces + 1),
         (chunks, 2, 2, 4), (chunks, 2, 2, 4), (chunks, 2, 2), (chunks, 2, 2),
-        (chunks,), (chunks, groups), (chunks, groups),
+        (chunks, 2), (chunks, groups), (chunks, groups),
     ]
     return tuple(pl.pallas_call(
         kernel,
@@ -373,6 +403,7 @@
         out_specs=(vmem, vmem),
         scratch_shapes=[
             pltpu.VMEM((chunks, supers, depth, LANES), bf16),
+            pltpu.VMEM((chunks, depth, LANES), bf16),
             pltpu.VMEM((chunks, depth, LANES), bf16),
             pltpu.VMEM((chunks, supers, rows_out, LANES), f32),
             pltpu.VMEM((chunks, 2, 2, 4, quarter, LANES), f32),
@@ -389,7 +420,7 @@
         cost_estimate=pl.CostEstimate(
             flops=2 * rows_out * depth * supers * block, bytes_accessed=8 * 2**20, transcendentals=0
         ),
-    )(pattern, ancestor_inverse, panels, diag_inverse))
+    )(turned, ancestor_inverse, panels, diag_inverse))
 
 
 def solution(mesh):

time: 192 us -> 159 us (0.83)
  Pallas kernels: 186 us -> 155 us
    pallas_call x1, Pallas kernels: 186 us -> 155 us  [local(): pl.pallas_call(kernel, out_shape=(jax.ShapeDtypeStruct((rows_out, width),...]
    unnamed x5 -> x4, local copies, waits for them, and re-layouts: 4.41 us -> 3.01 us
where the time goes in v2:
time: 159 us
  Pallas kernels  155 us (97%)
  local copies, waits for them, and re-layouts  3.01 us (2%)
    pallas_call x1, Pallas kernels, local(): pl.pallas_call(kernel, out_shape=(jax.ShapeDtypeStruct((rows_out, width),...  155 us

profile of v2, /device:TPU:1, one launch (start us, length us, event | category | flops | bytes accessed | tf_op | source)
XLA Modules:
  0.0 159.0 jit_solution(8253284709049523976)
XLA Ops:
  0.6 155.4 %shard_map.59 = (f32[1024,256]{1,0:T(8,128)}, f32[1,256,256]{2,1,0:T(8,128)}) custom-call(s32[16,64]{1,0:T(8,128)} %bitcast.1, bf16[1024,1024]{1,0:T(8,128)(2,1)} %a_ref.1, bf16[1024,256]{1,0:T(8,128)(2,1)} %panel.1, f32[1,256,256]{2,1,0:T(8,128)} %dinv.1), custom_call_target="tpu_custom_call" | custom-call | flops 8589934592 | bytes 8388608 | tf_op jit(solution)/shard_map/pallas_call | solution.py:396
  156.0 0.0 copy-start
  156.0 2.3 %copy.8 = f32[1024,256]{1,0:T(8,128)} copy(f32[1024,256]{1,0:T(8,128)} %get-tuple-element.4) | data formatting | bytes 2097152
  158.3 0.0 copy-done
  158.3 0.7 copy.9
Async XLA Ops:
  156.0 2.3 %copy-start = (f32[1,256,256]{2,1,0:T(8,128)S(1)}, f32[1,256,256]{2,1,0:T(8,128)}, u32[]{:S(2)}) copy-start(f32[1,256,256]{2,1,0:T(8,128)} %get-tuple-element.5) | copy-start | bytes 786436

commit v3 on v2

--- a/solution.py
+++ b/solution.py
@@ -8,12 +8,14 @@
 MESH = pl.DeviceIdType.MESH
 SIDE = 4
 LANES = 128
+TOP = 32000.0
+PER_NAT = 180.0
 OFFSETS = (2, 1, 3, 0)
 
 
 def kernel(
     pattern, a_ref, panel, dinv, cov, diag,
-    mbuf, match, relay, pbuf, r1, r2, r3, r4, term, dpart, dsum,
+    mbuf, match, relay, pbuf, e1, r1, e2, r2, e3, r3, e4, r4, term, dpart, dsum,
     zs, zr, ls, lr, s1, q1, s2, q2, s3, q3, s4, q4, ts, tr, ps, pr, bs, br,
 ):
     nz = lax.axis_size("col")
@@ -163,41 +165,63 @@
         s = b * SIDE + a if f == 0 else a * SIDE + b
         return pbuf.at[c, s, pl.ds(f * half + lo, n), :]
 
+    def encode(to, value):
+        n = value.shape[0]
+        shaped = value.reshape(2, n // 16, 8, LANES)
+        largest = jnp.max(jnp.abs(shaped), axis=1).reshape(16, LANES)
+        level = jnp.ceil(jnp.log(jnp.maximum(largest, 1e-30)) * PER_NAT)
+        to[pl.ds(0, 16), :] = level.astype(jnp.int32).astype(jnp.int16)
+        factor = (TOP * jnp.exp(level * (-1.0 / PER_NAT))).reshape(2, 1, 8, LANES)
+        rounded = jnp.round(shaped * factor).reshape(n, LANES)
+        to[pl.ds(16, n), :] = rounded.astype(jnp.int32).astype(jnp.int16)
+
+    def decode(at):
+        n = at.shape[0] - 16
+        level = at[pl.ds(0, 16), :].astype(jnp.int32).astype(jnp.float32)
+        factor = (jnp.exp(level * (1.0 / PER_NAT)) * (1.0 / TOP)).reshape(2, 1, 8, LANES)
+        value = at[pl.ds(16, n), :].astype(jnp.int32).astype(jnp.float32)
+        return (value.reshape(2, n // 16, 8, LANES) * factor).reshape(n, LANES)
+
     def far(c, f, way, k):
         return remote(
-            part(c, f, 2, k, way * quarter, quarter), r1.at[c, f, way, k],
+            e1.at[c, f, way, k], r1.at[c, f, way, k],
             s1.at[c, f, way, k], q1.at[c, f, way, k], dev_first(f, 1 - 2 * way),
         )
 
     def near(c, f, way, k):
         return remote(
-            part(c, f, 1 + 2 * way, k, 0, half), r2.at[c, f, way, k],
+            e2.at[c, f, way, k], r2.at[c, f, way, k],
             s2.at[c, f, way, k], q2.at[c, f, way, k], dev_first(f, 1 - 2 * way),
         )
 
     def far_second(c, f, way):
         return remote(
-            part(c, f, 0, 0, way * quarter, quarter), r3.at[c, f, way],
+            e3.at[c, f, way], r3.at[c, f, way],
             s3.at[c, f, way], q3.at[c, f, way], dev_second(f, 1 - 2 * way),
         )
 
     def near_second(c, f, way):
         return remote(
-            part(c, f, 0, 1 + way, 0, half), r4.at[c, f, way],
+            e4.at[c, f, way], r4.at[c, f, way],
             s4.at[c, f, way], q4.at[c, f, way], dev_second(f, 1 - 2 * way),
         )
+
+    def joined(value, add, way):
+        low, high = value[:quarter], value[quarter:]
+        return jnp.concatenate([low + add, high] if way == 0 else [low, high + add], axis=0)
 
     def send_far(c, k):
         for f in range(2):
             for way in range(2):
+                encode(e1.at[c, f, way, k], part(c, f, 2, k, way * quarter, quarter)[...])
                 far(c, f, way, k).start()
 
     def send_near(c, k):
         for f in range(2):
             for way in range(2):
                 far(c, f, way, k).wait_recv()
-                own = part(c, f, 1 + 2 * way, k, way * quarter, quarter)
-                own[...] = own[...] + r1[c, f, way, k]
+                own = part(c, f, 1 + 2 * way, k, 0, half)[...]
+                encode(e2.at[c, f, way, k], joined(own, decode(r1.at[c, f, way, k]), way))
                 near(c, f, way, k).start()
 
     def turn(c, k):
@@ -205,16 +229,18 @@
             for way in range(2):
                 near(c, f, way, k).wait_recv()
             own = part(c, f, 0, k, 0, half)
-            own[...] = own[...] + (r2[c, f, 0, k] + r2[c, f, 1, k])
+            total = own[...] + (decode(r2.at[c, f, 0, k]) + decode(r2.at[c, f, 1, k]))
             if k == 0:
-                far_second(c, f, 0).start()
-                far_second(c, f, 1).start()
+                for way in range(2):
+                    encode(e3.at[c, f, way], total[way * quarter:(way + 1) * quarter])
+                    far_second(c, f, way).start()
             elif k < 3:
                 way = k - 1
                 far_second(c, f, way).wait_recv()
-                own = part(c, f, 0, k, way * quarter, quarter)
-                own[...] = own[...] + r3[c, f, way]
+                encode(e4.at[c, f, way], joined(total, decode(r3.at[c, f, way]), way))
                 near_second(c, f, way).start()
+            else:
+                own[...] = total
 
     def swap(c):
         return remote(mbuf.at[c, held], relay.at[c], ts.at[c, 0], tr.at[c, 0], taker)
@@ -249,7 +275,7 @@
             for way in range(2):
                 near_second(c, f, way).wait_recv()
             own = part(c, f, 0, 3, 0, half)
-            own[...] = own[...] + (r4[c, f, 0] + r4[c, f, 1])
+            own[...] = own[...] + (decode(r4.at[c, f, 0]) + decode(r4.at[c, f, 1]))
         product = pbuf.at[c, row]
 
         if c == 0:
@@ -388,6 +414,10 @@
     pieces = 2 * (nz // 2) - 1
     dma = pltpu.SemaphoreType.DMA
     vmem = pl.BlockSpec(memory_space=pltpu.VMEM)
+    sums = [
+        (chunks, 2, 2, 4, quarter + 16, LANES), (chunks, 2, 2, 4, half + 16, LANES),
+        (chunks, 2, 2, quarter + 16, LANES), (chunks, 2, 2, half + 16, LANES),
+    ]
     sems = [
         (chunks, 2, pieces), (chunks, 2 * pieces + 1),
         (chunks, 2, 2, 4), (chunks, 2, 2, 4), (chunks, 2, 2), (chunks, 2, 2),
@@ -406,10 +436,7 @@
             pltpu.VMEM((chunks, depth, LANES), bf16),
             pltpu.VMEM((chunks, depth, LANES), bf16),
             pltpu.VMEM((chunks, supers, rows_out, LANES), f32),
-            pltpu.VMEM((chunks, 2, 2, 4, quarter, LANES), f32),
-            pltpu.VMEM((chunks, 2, 2, 4, half, LANES), f32),
-            pltpu.VMEM((chunks, 2, 2, quarter, LANES), f32),
-            pltpu.VMEM((chunks, 2, 2, half, LANES), f32),
+        ] + [pltpu.VMEM(s, jnp.int16) for s in sums for _ in range(2)] + [
             pltpu.VMEM((chunks, block, LANES), f32),
             pltpu.VMEM((chunks, groups, block // groups, LANES), f32),
             pltpu.VMEM((chunks, block, LANES), f32),

time: 159 us -> 122 us (0.77)
  Pallas kernels: 155 us -> 119 us
    pallas_call x1, Pallas kernels: 155 us -> 119 us  [local(): pl.pallas_call(kernel, out_shape=(jax.ShapeDtypeStruct((rows_out, width),...]
where the time goes in v3:
time: 122 us
  Pallas kernels  119 us (98%)
  local copies, waits for them, and re-layouts  3.01 us (2%)
    pallas_call x1, Pallas kernels, local(): pl.pallas_call(kernel, out_shape=(jax.ShapeDtypeStruct((rows_out, width),...  119 us
    unnamed x4, local copies, waits for them, and re-layouts  3.01 us

profile of v3, /device:TPU:1, one launch (start us, length us, event | category | flops | bytes accessed | tf_op | source)
XLA Modules:
  0.0 122.3 jit_solution(5733444125625271993)
XLA Ops:
  0.6 118.6 %shard_map.59 = (f32[1024,256]{1,0:T(8,128)}, f32[1,256,256]{2,1,0:T(8,128)}) custom-call(s32[16,64]{1,0:T(8,128)} %bitcast.1, bf16[1024,1024]{1,0:T(8,128)(2,1)} %a_ref.1, bf16[1024,256]{1,0:T(8,128)(2,1)} %panel.1, f32[1,256,256]{2,1,0:T(8,128)} %dinv.1), custom_call_target="tpu_custom_call" | custom-call | flops 8589934592 | bytes 8388608 | tf_op jit(solution)/shard_map/pallas_call | solution.py:426
  119.3 0.0 copy-start
  119.3 2.3 %copy.8 = f32[1024,256]{1,0:T(8,128)} copy(f32[1024,256]{1,0:T(8,128)} %get-tuple-element.4) | data formatting | bytes 2097152
  121.6 0.0 copy-done
  121.6 0.7 copy.9
Async XLA Ops:
  119.3 2.3 %copy-start = (f32[1,256,256]{2,1,0:T(8,128)S(1)}, f32[1,256,256]{2,1,0:T(8,128)}, u32[]{:S(2)}) copy-start(f32[1,256,256]{2,1,0:T(8,128)} %get-tuple-element.5) | copy-start | bytes 786436

commit v4 on v3

--- a/solution.py
+++ b/solution.py
@@ -15,8 +15,8 @@
 
 def kernel(
     pattern, a_ref, panel, dinv, cov, diag,
-    mbuf, match, relay, pbuf, e1, r1, e2, r2, e3, r3, e4, r4, term, dpart, dsum,
-    zs, zr, ls, lr, s1, q1, s2, q2, s3, q3, s4, q4, ts, tr, ps, pr, bs, br,
+    mbuf, match, relay, pbuf, e1, r1, e2, r2, e3, r3, e4, r4, term, traded, dpart, dsum,
+    zs, zr, ls, lr, s1, q1, s2, q2, s3, q3, s4, q4, ts, tr, ds, dr, ps, pr, bs, br,
 ):
     nz = lax.axis_size("col")
     leaf = lax.axis_index("leaf")
@@ -34,10 +34,6 @@
     chunks = block // LANES
     piece = block // groups
 
-    def peer(j):
-        p = lax.rem(group + j, groups)
-        return (p // nz, row, lax.rem(p, nz))
-
     def z_dev(step):
         return (leaf, row, lax.rem(z + step + nz, nz))
 
@@ -64,11 +60,11 @@
 
     barrier = pltpu.get_barrier_semaphore()
 
-    @pl.loop(1, groups)
+    @pl.loop(1, nz)
     def _(j):
-        pl.semaphore_signal(barrier, inc=1, device_id=peer(j), device_id_type=MESH)
-
-    for dev in (x_dev(1), x_dev(-1), y_dev(1), y_dev(-1)):
+        pl.semaphore_signal(barrier, inc=1, device_id=z_dev(j), device_id_type=MESH)
+
+    for dev in (other, x_dev(1), x_dev(-1), y_dev(1), y_dev(-1)):
         pl.semaphore_signal(barrier, inc=1, device_id=dev, device_id_type=MESH)
 
     @pl.when(moves)
@@ -82,7 +78,7 @@
             values = panel[rows, pl.ds(c * LANES, LANES)].astype(jnp.float32) * keep
             mbuf[c, group, rows, :] = values.astype(jnp.bfloat16)
 
-    pl.semaphore_wait(barrier, groups - 1 + 4 + moves.astype(jnp.int32))
+    pl.semaphore_wait(barrier, nz + 4 + moves.astype(jnp.int32))
 
     turns = nz // 2
     pieces = 2 * turns - 1
@@ -123,13 +119,10 @@
                 leaf_copy(c, way, j, leaf).start()
 
     def multiply(c, sa, sb):
-        @pl.loop(0, a_ref.shape[0] // 256)
-        def _(t):
-            rows = pl.ds(pl.multiple_of(t * 256, 256), 256)
-            right = jnp.concatenate([mbuf[c, sa], mbuf[c, sb]], axis=1)
-            out = jnp.dot(a_ref[rows, :], right, preferred_element_type=jnp.float32)
-            pbuf[c, sa, rows, :] = out[:, :LANES]
-            pbuf[c, sb, rows, :] = out[:, LANES:]
+        right = jnp.concatenate([mbuf[c, sa], mbuf[c, sb]], axis=1)
+        out = jnp.dot(a_ref[...], right, preferred_element_type=jnp.float32)
+        pbuf[c, sa] = out[:, :LANES]
+        pbuf[c, sb] = out[:, LANES:]
 
     def products(c, d):
         if d == 0:
@@ -159,11 +152,16 @@
     def dev_second(f, step):
         return (y_dev, x_dev)[f](step)
 
-    def part(c, f, df, k, lo, n):
-        a = lax.rem(first(f) + df, SIDE)
-        b = lax.rem(second(f) + OFFSETS[k], SIDE)
-        s = b * SIDE + a if f == 0 else a * SIDE + b
-        return pbuf.at[c, s, pl.ds(f * half + lo, n), :]
+    def quarter_of(c, s, f, q):
+        return pbuf.at[c, s, pl.ds(pl.multiple_of(f * half + q * quarter, quarter), quarter), :]
+
+    def own_block(f, k):
+        t = lax.rem(second(f) + OFFSETS[k], SIDE)
+        return t, (t * SIDE + x if f == 0 else y * SIDE + t)
+
+    def place(f, s):
+        a, b = (lax.rem(s, SIDE), s // SIDE)[::1 - 2 * f]
+        return lax.rem(a - first(f) + SIDE, SIDE), b
 
     def encode(to, value):
         n = value.shape[0]
@@ -182,16 +180,16 @@
         value = at[pl.ds(16, n), :].astype(jnp.int32).astype(jnp.float32)
         return (value.reshape(2, n // 16, 8, LANES) * factor).reshape(n, LANES)
 
-    def far(c, f, way, k):
+    def far(c, f, way, t):
         return remote(
-            e1.at[c, f, way, k], r1.at[c, f, way, k],
-            s1.at[c, f, way, k], q1.at[c, f, way, k], dev_first(f, 1 - 2 * way),
-        )
-
-    def near(c, f, way, k):
+            e1.at[c, f, way, t], r1.at[c, f, way, t],
+            s1.at[c, f, way, t], q1.at[c, f, way, t], dev_first(f, 1 - 2 * way),
+        )
+
+    def near(c, f, way, t):
         return remote(
-            e2.at[c, f, way, k], r2.at[c, f, way, k],
-            s2.at[c, f, way, k], q2.at[c, f, way, k], dev_first(f, 1 - 2 * way),
+            e2.at[c, f, way, t], r2.at[c, f, way, t],
+            s2.at[c, f, way, t], q2.at[c, f, way, t], dev_first(f, 1 - 2 * way),
         )
 
     def far_second(c, f, way):
@@ -206,41 +204,58 @@
             s4.at[c, f, way], q4.at[c, f, way], dev_second(f, 1 - 2 * way),
         )
 
-    def joined(value, add, way):
-        low, high = value[:quarter], value[quarter:]
-        return jnp.concatenate([low + add, high] if way == 0 else [low, high + add], axis=0)
-
-    def send_far(c, k):
-        for f in range(2):
-            for way in range(2):
-                encode(e1.at[c, f, way, k], part(c, f, 2, k, way * quarter, quarter)[...])
-                far(c, f, way, k).start()
+    def arrived(d, act):
+        both = 1 if d in (0, turns) else 2
+
+        @pl.loop(0, 2 * both)
+        def _(i):
+            step = d if both == 1 else d * (1 - 2 * lax.rem(i, 2))
+            act((i // both) * nz + lax.rem(z + step + nz, nz))
+
+    def send_far(c, d):
+        def act(s):
+            for f in range(2):
+                ahead, t = place(f, s)
+
+                @pl.when(ahead == 2)
+                def _():
+                    for way in range(2):
+                        encode(e1.at[c, f, way, t], quarter_of(c, s, f, way)[...])
+                        far(c, f, way, t).start()
+
+        arrived(d, act)
 
     def send_near(c, k):
         for f in range(2):
-            for way in range(2):
-                far(c, f, way, k).wait_recv()
-                own = part(c, f, 1 + 2 * way, k, 0, half)[...]
-                encode(e2.at[c, f, way, k], joined(own, decode(r1.at[c, f, way, k]), way))
-                near(c, f, way, k).start()
+            t = lax.rem(second(f) + OFFSETS[k], SIDE)
+            for way in range(2):
+                a = lax.rem(first(f) + 1 + 2 * way, SIDE)
+                s = t * SIDE + a if f == 0 else a * SIDE + t
+                encode(e2.at[c, f, way, t, 1 - way], quarter_of(c, s, f, 1 - way)[...])
+                far(c, f, way, t).wait_recv()
+                value = quarter_of(c, s, f, way)[...] + decode(r1.at[c, f, way, t])
+                encode(e2.at[c, f, way, t, way], value)
+                near(c, f, way, t).start()
 
     def turn(c, k):
         for f in range(2):
-            for way in range(2):
-                near(c, f, way, k).wait_recv()
-            own = part(c, f, 0, k, 0, half)
-            total = own[...] + (decode(r2.at[c, f, 0, k]) + decode(r2.at[c, f, 1, k]))
+            t, s = own_block(f, k)
+            for way in range(2):
+                near(c, f, way, t).wait_recv()
+            for q in range(2):
+                own = quarter_of(c, s, f, q)
+                own[...] = own[...] + (decode(r2.at[c, f, 0, t, q]) + decode(r2.at[c, f, 1, t, q]))
             if k == 0:
                 for way in range(2):
-                    encode(e3.at[c, f, way], total[way * quarter:(way + 1) * quarter])
+                    encode(e3.at[c, f, way], quarter_of(c, s, f, way)[...])
                     far_second(c, f, way).start()
             elif k < 3:
                 way = k - 1
+                encode(e4.at[c, f, way, 1 - way], quarter_of(c, s, f, 1 - way)[...])
                 far_second(c, f, way).wait_recv()
-                encode(e4.at[c, f, way], joined(total, decode(r3.at[c, f, way]), way))
+                value = quarter_of(c, s, f, way)[...] + decode(r3.at[c, f, way])
+                encode(e4.at[c, f, way, way], value)
                 near_second(c, f, way).start()
-            else:
-                own[...] = total
 
     def swap(c):
         return remote(mbuf.at[c, held], relay.at[c], ts.at[c, 0], tr.at[c, 0], taker)
@@ -274,20 +289,24 @@
         for f in range(2):
             for way in range(2):
                 near_second(c, f, way).wait_recv()
-            own = part(c, f, 0, 3, 0, half)
-            own[...] = own[...] + (decode(r4.at[c, f, 0]) + decode(r4.at[c, f, 1]))
+            for q in range(2):
+                own = quarter_of(c, row, f, q)
+                own[...] = own[...] + (decode(r4.at[c, f, 0, q]) + decode(r4.at[c, f, 1, q]))
         product = pbuf.at[c, row]
-
-        if c == 0:
-            @pl.when(goes_on)
-            def _():
-                for e in range(chunks):
-                    swap_on(e).wait_recv()
-
-        value = product[...]
+        for i in range(blocks):
+            keep = pattern[row, group * blocks + i].astype(jnp.float32)
+            rows = pl.ds(i * block, block)
+            cov[rows, pl.ds(c * LANES, LANES)] = -(product[rows, :] * keep)
+
+    def diag_terms():
+        @pl.when(goes_on)
+        def _():
+            for c in range(chunks):
+                swap_on(c).wait_recv()
+
+        columns = jnp.concatenate([match[c] for c in range(chunks)], axis=1)
+        rest = jnp.concatenate([pbuf[c, row] for c in range(chunks)], axis=1)
         total = None
-        rest = value
-        columns = jnp.concatenate([match[e] for e in range(chunks)], axis=1)
         for _ in range(3):
             top = rest.astype(jnp.bfloat16)
             rest = rest - top.astype(jnp.float32)
@@ -295,83 +314,90 @@
                 columns, top, (((0,), (0,)), ((), ())), preferred_element_type=jnp.float32
             )
             total = add if total is None else total + add
-        term[c] = total
-
-        @pl.loop(1, groups)
+        term[...] = total
+
+    wide = block // 2
+
+    def side(lf):
+        return pl.ds(pl.multiple_of(lf * wide, wide), wide)
+
+    def mine(owner):
+        return pl.ds(pl.multiple_of(leaf * wide + owner * piece, piece), piece)
+
+    def trade():
+        return remote(term.at[side(1 - leaf), :], traded, ds.at[0], dr.at[0], other)
+
+    def give(j):
+        return remote(
+            term.at[mine(lax.rem(z + j, nz)), :], dpart.at[j], ps.at[j], pr.at[j], z_dev(j)
+        )
+
+    def spread(j, owner):
+        view = dsum.at[mine(owner), :]
+        return remote(view, view, bs.at[j], br.at[j], z_dev(j))
+
+    def hand(lf):
+        view = dsum.at[side(lf), :]
+        return remote(view, view, ds.at[1], dr.at[1], other)
+
+    def diag_sum():
+        trade().start()
+        trade().wait_recv()
+        term[side(leaf), :] = term[side(leaf), :] + traded[...]
+
+        @pl.loop(1, nz)
         def _(j):
-            give(c, j).start()
-
-        for i in range(blocks):
-            keep = pattern[row, group * blocks + i].astype(jnp.float32)
-            rows = pl.ds(i * block, block)
-            cov[rows, pl.ds(c * LANES, LANES)] = -(product[rows, :] * keep)
-
-    def give(c, j):
-        to = lax.rem(group + j, groups)
-        rows = pl.ds(pl.multiple_of(to * piece, piece), piece)
-        return remote(term.at[c, rows, :], dpart.at[c, j], ps.at[c, j], pr.at[c, j], peer(j))
-
-    def mine(owner):
-        return pl.ds(pl.multiple_of(owner * piece, piece), piece)
-
-    def spread(c, j, owner):
-        view = dsum.at[c, mine(owner), :]
-        return remote(view, view, bs.at[c, j], br.at[c, j], peer(j))
-
-    def settle(c):
-        @pl.loop(1, groups)
+            give(j).start()
+
+        @pl.loop(1, nz)
         def _(j):
-            give(c, j).wait_recv()
-
-        dsum[c, mine(group), :] = (
-            dinv[0, mine(group), pl.ds(c * LANES, LANES)]
-            + (term[c, mine(group), :] + jnp.sum(dpart[c, pl.ds(1, groups - 1)], axis=0))
-        )
-
-        @pl.loop(1, groups)
+            give(j).wait_recv()
+
+        dsum[mine(z), :] = dinv[0, mine(z), :] + (
+            term[mine(z), :] + jnp.sum(dpart[pl.ds(1, nz - 1)], axis=0)
+        )
+
+        @pl.loop(1, nz)
         def _(j):
-            spread(c, j, group).start()
-
-    def collect(c):
-        @pl.loop(1, groups)
+            spread(j, z).start()
+
+        @pl.loop(1, nz)
         def _(j):
-            spread(c, j, lax.rem(group - j + groups, groups)).wait_recv()
-
-        diag[0, :, pl.ds(c * LANES, LANES)] = dsum[c]
+            spread(j, lax.rem(z - j + nz, nz)).wait_recv()
+
+        hand(leaf).start()
+        hand(1 - leaf).wait_recv()
+        diag[0] = dsum[...]
 
     gather_begin(0)
-    products(0, 0)
     for d in range(turns):
         gather_step(0, d)
         if d == turns - 2:
             gather_begin(1)
-        if d > 0:
-            products(0, d)
+        products(0, d)
+        send_far(0, d)
     products(0, turns)
-    for k in range(4):
-        send_far(0, k)
+    send_far(0, turns)
     send_match(0)
-    products(1, 0)
-    for k in range(4):
-        gather_step(1, k)
-        send_near(0, k)
-        products(1, k + 1)
+    for d in range(turns):
+        gather_step(1, d)
+        send_near(0, d)
+        products(1, d)
+        send_far(1, d)
+    products(1, turns)
+    send_far(1, turns)
+    send_match(1)
     pass_match(0)
-    for k in range(4):
-        send_far(1, k)
-    send_match(1)
-    for k in range(4):
+    for k in range(SIDE):
         turn(0, k)
         send_near(1, k)
+    finish(0)
     pass_match(1)
-    finish(0)
-    for k in range(4):
+    for k in range(SIDE):
         turn(1, k)
-    settle(0)
     finish(1)
-    collect(0)
-    settle(1)
-    collect(1)
+    diag_terms()
+    diag_sum()
 
     for c in range(chunks):
         leaf_own(c, leaf).wait_send()
@@ -386,11 +412,6 @@
                 far_second(c, f, way).wait_send()
                 near_second(c, f, way).wait_send()
 
-        @pl.loop(1, groups)
-        def _(j):
-            give(c, j).wait_send()
-            spread(c, j, group).wait_send()
-
         @pl.when(moves)
         def _():
             swap(c).wait_send()
@@ -398,6 +419,14 @@
         @pl.when(goes_on)
         def _():
             swap_on(c).wait_send()
+
+    trade().wait_send()
+    hand(leaf).wait_send()
+
+    @pl.loop(1, nz)
+    def _(j):
+        give(j).wait_send()
+        spread(j, z).wait_send()
 
 
 def local(ancestor_inverse, panels, pattern, diag_inverse):
@@ -415,13 +444,13 @@
     dma = pltpu.SemaphoreType.DMA
     vmem = pl.BlockSpec(memory_space=pltpu.VMEM)
     sums = [
-        (chunks, 2, 2, 4, quarter + 16, LANES), (chunks, 2, 2, 4, half + 16, LANES),
-        (chunks, 2, 2, quarter + 16, LANES), (chunks, 2, 2, half + 16, LANES),
+        (chunks, 2, 2, 4, quarter + 16, LANES), (chunks, 2, 2, 4, 2, quarter + 16, LANES),
+        (chunks, 2, 2, quarter + 16, LANES), (chunks, 2, 2, 2, quarter + 16, LANES),
     ]
     sems = [
         (chunks, 2, pieces), (chunks, 2 * pieces + 1),
         (chunks, 2, 2, 4), (chunks, 2, 2, 4), (chunks, 2, 2), (chunks, 2, 2),
-        (chunks, 2), (chunks, groups), (chunks, groups),
+        (chunks, 2), (2,), (nz,), (nz,),
     ]
     return tuple(pl.pallas_call(
         kernel,
@@ -437,9 +466,10 @@
             pltpu.VMEM((chunks, depth, LANES), bf16),
             pltpu.VMEM((chunks, supers, rows_out, LANES), f32),
         ] + [pltpu.VMEM(s, jnp.int16) for s in sums for _ in range(2)] + [
-            pltpu.VMEM((chunks, block, LANES), f32),
-            pltpu.VMEM((chunks, groups, block // groups, LANES), f32),
-            pltpu.VMEM((chunks, block, LANES), f32),
+            pltpu.VMEM((block, block), f32),
+            pltpu.VMEM((block // 2, block), f32),
+            pltpu.VMEM((nz, block // groups, block), f32),
+            pltpu.VMEM((block, block), f32),
         ] + [dma(s) for s in sems for _ in range(2)],
         compiler_params=pltpu.CompilerParams(
             collective_id=0, has_side_effects=True, vmem_limit_bytes=58 * 2**20

time: 122 us -> 116 us (0.951)
  Pallas kernels: 119 us -> 112 us
    pallas_call x1, Pallas kernels: 119 us -> 112 us  [local(): pl.pallas_call(kernel, out_shape=(jax.ShapeDtypeStruct((rows_out, width),...]
where the time goes in v4:
time: 116 us
  Pallas kernels  112 us (97%)
  local copies, waits for them, and re-layouts  3.01 us (3%)
    pallas_call x1, Pallas kernels, local(): pl.pallas_call(kernel, out_shape=(jax.ShapeDtypeStruct((rows_out, width),...  112 us
    unnamed x4, local copies, waits for them, and re-layouts  3.01 us

profile of v4, /device:TPU:1, one launch (start us, length us, event | category | flops | bytes accessed | tf_op | source)
XLA Modules:
  0.0 116.0 jit_solution(16118353410631097084)
XLA Ops:
  0.6 112.4 %shard_map.59 = (f32[1024,256]{1,0:T(8,128)}, f32[1,256,256]{2,1,0:T(8,128)}) custom-call(s32[16,64]{1,0:T(8,128)} %bitcast.1, bf16[1024,1024]{1,0:T(8,128)(2,1)} %a_ref.1, bf16[1024,256]{1,0:T(8,128)(2,1)} %panel.1, f32[1,256,256]{2,1,0:T(8,128)} %dinv.1), custom_call_target="tpu_custom_call" | custom-call | flops 8589934592 | bytes 8388608 | tf_op jit(solution)/shard_map/pallas_call | solution.py:455
  113.0 0.0 copy-start
  113.0 2.3 %copy.8 = f32[1024,256]{1,0:T(8,128)} copy(f32[1024,256]{1,0:T(8,128)} %get-tuple-element.4) | data formatting | bytes 2097152
  115.3 0.0 copy-done
  115.3 0.7 copy.9
Async XLA Ops:
  113.0 2.3 %copy-start = (f32[1,256,256]{2,1,0:T(8,128)S(1)}, f32[1,256,256]{2,1,0:T(8,128)}, u32[]{:S(2)}) copy-start(f32[1,256,256]{2,1,0:T(8,128)} %get-tuple-element.5) | copy-start | bytes 786436

commit v5 on v4

--- a/solution.py
+++ b/solution.py
@@ -292,6 +292,8 @@
             for q in range(2):
                 own = quarter_of(c, row, f, q)
                 own[...] = own[...] + (decode(r4.at[c, f, 0, q]) + decode(r4.at[c, f, 1, q]))
+
+    def write_covariance(c):
         product = pbuf.at[c, row]
         for i in range(blocks):
             keep = pattern[row, group * blocks + i].astype(jnp.float32)
@@ -348,6 +350,9 @@
         @pl.loop(1, nz)
         def _(j):
             give(j).start()
+
+        for c in range(chunks):
+            write_covariance(c)
 
         @pl.loop(1, nz)
         def _(j):

time: 116 us -> 116 us (level)
  no operation moved by 1% of the time
where the time goes in v5:
time: 116 us
  Pallas kernels  112 us (97%)
  local copies, waits for them, and re-layouts  3.01 us (3%)
    pallas_call x1, Pallas kernels, local(): pl.pallas_call(kernel, out_shape=(jax.ShapeDtypeStruct((rows_out, width),...  112 us
    unnamed x4, local copies, waits for them, and re-layouts  3.01 us

profile of v5, /device:TPU:1, one launch (start us, length us, event | category | flops | bytes accessed | tf_op | source)
XLA Modules:
  0.0 116.0 jit_solution(12074267128716121021)
XLA Ops:
  0.6 112.3 %shard_map.59 = (f32[1024,256]{1,0:T(8,128)}, f32[1,256,256]{2,1,0:T(8,128)}) custom-call(s32[16,64]{1,0:T(8,128)} %bitcast.1, bf16[1024,1024]{1,0:T(8,128)(2,1)} %a_ref.1, bf16[1024,256]{1,0:T(8,128)(2,1)} %panel.1, f32[1,256,256]{2,1,0:T(8,128)} %dinv.1), custom_call_target="tpu_custom_call" | custom-call | flops 8589934592 | bytes 8388608 | tf_op jit(solution)/shard_map/pallas_call | solution.py:460
  113.0 0.0 copy-start
  113.0 2.3 %copy.8 = f32[1024,256]{1,0:T(8,128)} copy(f32[1024,256]{1,0:T(8,128)} %get-tuple-element.4) | data formatting | bytes 2097152
  115.3 0.0 copy-done
  115.3 0.7 copy.9
Async XLA Ops:
  113.0 2.3 %copy-start = (f32[1,256,256]{2,1,0:T(8,128)S(1)}, f32[1,256,256]{2,1,0:T(8,128)}, u32[]{:S(2)}) copy-start(f32[1,256,256]{2,1,0:T(8,128)} %get-tuple-element.5) | copy-start | bytes 786436
